TPU v7x, 512 devices: a whole 4x4x16 slice. The times are simulated.
512 devices in a mesh: mem: 16 (over y_lo, x, core), lat: 32 (over y_hi, z).
Axes of the slice: x: 4, y: 4 (y_hi: 2, y_lo: 2; y = y_hi * 2 + y_lo), z: 16, core: 2. Of those that a mesh axis runs over, the one named last changes fastest.
Arguments:
- perturbation: bfloat16 [256, 512, 2048], P('mem', 'lat'), may hold values from -6 to 6
- obs_cells: int32 [32, 2048], P('lat'), may hold values from 0 to 32767
- obs_count: int32 [32], P('lat'), may hold values from 682 to 2048, as said below
- innovation: float32 [32, 2048], P('lat'), may hold values from -8 to 8
- obs_scale: float32 [32, 2048], P('lat'), may hold values from 0.3 to 3
Outputs:
- control: float32 [256, 256, 1024], P('mem', 'lat')
- increment: float32 [512, 2048], P('lat', 'mem')
Inputs may be any that keep to these rules, and one draw needn't show every extreme that they name: `obs_count`: at most 2048 live slots in a band, and some band has exactly 2048.
All inputs are finite; a program needn't handle non-finite values.
Results may differ from a plain program's by a relative error of at most 0.00035.
Values sent between devices are 32-bit elements; how exact they have to be, the bound alone decides.
A program may use at most 64 MiB of HBM per device.

v0:
```python
import functools

import jax
import jax.numpy as jnp
from jax import lax
from jax.sharding import Mesh
from jax.sharding import PartitionSpec as P

HALO = 8
LSIG = 3
ITERS = 3
MEM = ("mem_0", "mem_1", "mem_2")
LAT = ("lat_0", "lat_1")
MEM_LAT = ("mem_0", "mem_1", "mem_2", "lat_0", "lat_1")


def padded_2(block, sides, width):
    for axis, dim in sides:
        count = lax.axis_size(axis)
        forward = [(i, i + 1) for i in range(count - 1)]
        backward = [(target, source) for source, target in forward]
        low = lax.ppermute(
            lax.slice_in_dim(block, block.shape[dim] - width, None, axis=dim), axis, forward
        )
        high = lax.ppermute(lax.slice_in_dim(block, 0, width, axis=dim), axis, backward)
        block = jnp.concatenate([low, block, high], axis=dim)
    return block


def sent_to_all(value, axis):
    devices = lax.axis_size(axis)
    return lax.all_to_all(
        jnp.broadcast_to(value[None], (devices, *value.shape)), axis, 0, 0, tiled=True
    )


def over_copies(value, axis):
    return sent_to_all(value, axis).sum(axis=0)


def one_axis_at_a_time(value, axes):
    return functools.reduce(lax.psum, axes, value)


def cut_along(value, dim, devices):
    before, after = (value.shape[:dim], value.shape[dim + 1 :])
    return jnp.moveaxis(value.reshape(*before, devices, -1, *after), dim, 0)


def sent_and_summed(value, axis, dim):
    blocks = cut_along(value, dim, lax.axis_size(axis))
    arrived = lax.all_to_all(blocks, axis, split_axis=0, concat_axis=0, tiled=True)
    return arrived.sum(axis=0)


def lat_weights():
    offsets = jnp.arange(2 * HALO + 1).astype(jnp.float32) - HALO
    spread = HALO / 2.0
    return 0.5 * jnp.exp(-offsets * offsets / (2.0 * spread * spread))


def lon_weights(coarse_cols):
    columns = jnp.arange(coarse_cols)
    distance = jnp.abs(columns[:, None] - columns[None, :])
    distance = jnp.minimum(distance, coarse_cols - distance).astype(jnp.float32)
    return jnp.exp(-distance * distance / (2.0 * LSIG * LSIG))


def band_matrix(row_count, lat_taps):
    rows = jnp.arange(row_count)[:, None]
    columns = jnp.arange(row_count + 2 * HALO)[None, :]
    offset_grid = columns - rows
    matrix = jnp.zeros((row_count, row_count + 2 * HALO), jnp.float32)
    for offset in range(2 * HALO + 1):
        matrix = matrix + jnp.where(offset_grid == offset, lat_taps[offset], 0.0)
    return matrix


def widen_lon(coarse):
    odd_part = 0.5 * (coarse + jnp.roll(coarse, -1, axis=-1))
    return jnp.stack([coarse, odd_part], axis=-1).reshape(
        coarse.shape[:-1] + (2 * coarse.shape[-1],)
    )


def narrow_lon(fine):
    paired = fine.reshape(fine.shape[:-1] + (fine.shape[-1] // 2, 2))
    odd_part = paired[..., 1]
    return paired[..., 0] + 0.5 * odd_part + 0.5 * jnp.roll(odd_part, 1, axis=-1)


def on_device(perturbation, obs_cells, obs_count, innovation, obs_scale):
    mem_count = lax.axis_size(MEM)
    local_members, fine_rows, lon_cells = perturbation.shape
    coarse_rows = fine_rows // 2
    coarse_cols = lon_cells // 2
    member_scale = (local_members * mem_count - 1) ** (-0.5)
    lat_taps = lat_weights()
    banded = band_matrix(coarse_rows, lat_taps)
    circulant = lon_weights(coarse_cols)
    obs_index = obs_cells[0]
    row_index = obs_index // lon_cells
    col_index = obs_index % lon_cells
    active = jnp.arange(obs_index.shape[0]) < obs_count[0]
    is_first = lax.axis_index(MEM) == 0
    target = innovation[0]
    saturation = obs_scale[0]

    def smooth(coarse):
        padded = padded_2(coarse, ((LAT, 1),), HALO)
        return jnp.einsum(
            "ij,mjk->mik",
            banded,
            padded,
            precision=lax.Precision.HIGHEST,
            preferred_element_type=jnp.float32,
        )

    bend_mask = active & is_first
    increment = jnp.zeros((fine_rows, lon_cells), jnp.float32)
    control = jnp.zeros((local_members, coarse_rows, coarse_cols), jnp.float32)
    observed = jnp.zeros(obs_index.shape, jnp.float32)
    for iteration in range(ITERS):
        misfit = target - observed
        bounded = jnp.tanh(misfit / saturation)
        pull = jnp.where(active, saturation * bounded, 0.0)
        weight = jnp.where(bend_mask, 1.0 - bounded * bounded, 0.0)
        obs_field = (
            jnp.zeros((fine_rows * lon_cells,), jnp.float32)
            .at[obs_index]
            .add(pull)
            .reshape(fine_rows, lon_cells)
        )
        weighted = perturbation.astype(jnp.float32) * obs_field[None] * member_scale
        folded = narrow_lon(weighted.reshape(local_members, coarse_rows, 2, lon_cells).sum(axis=2))
        gradient = control - smooth(
            jnp.dot(
                folded,
                circulant,
                precision=lax.Precision.HIGHEST,
                preferred_element_type=jnp.float32,
            )
        )
        local_norm = jnp.sum(gradient * gradient)
        direction = -gradient
        smoothed = smooth(direction)
        along = jnp.dot(
            smoothed, circulant, precision=lax.Precision.HIGHEST, preferred_element_type=jnp.float32
        )
        fine_block = jnp.repeat(widen_lon(along), 2, axis=1)
        partial_image = (
            jnp.sum(perturbation.astype(jnp.float32) * fine_block, axis=0) * member_scale
        )
        hits = over_copies(partial_image[row_index, col_index], MEM)
        local_bend = jnp.sum(weight * hits * hits)
        grad_norm, bending = (
            one_axis_at_a_time(local_norm, MEM_LAT),
            one_axis_at_a_time(local_bend, MEM_LAT),
        )
        step_size = grad_norm / (grad_norm + bending + 1e-06)
        control = control + step_size * direction
        increment = increment + step_size * partial_image
        observed = observed + step_size * hits
    increment = sent_and_summed(increment, MEM, 1)
    return (control, increment)


def solution(mesh):
    split = Mesh(
        mesh.devices.reshape(2, 4, 2, 2, 16), ("mem_0", "mem_1", "mem_2", "lat_0", "lat_1")
    )
    placed = (P(MEM, LAT, None), P(LAT, None), P(LAT), P(LAT, None), P(LAT, None))
    return jax.shard_map(
        on_device,
        mesh=split,
        in_specs=placed,
        out_specs=(P(MEM, LAT, None), P(LAT, MEM)),
        check_vma=False,
    )
```

profile of v0, /device:TPU:1, one launch (start us, length us, event | category | flops | bytes accessed | tf_op | source)
XLA Modules:
  0.0 598.7 jit_solution(3824614258439709847)
XLA Ops:
  2.8 11.3 %scatter_custom_fusion = f32[32768]{0:T(1024)S(1)} fusion(s32[2048]{0:T(1024)S(1)} %bitcast.175, f32[2048]{0:T(1024)S(1)} %multiply_select_fusion.2, f32[]{:T(128)} %constant.35.clone.1), kind=kCustom, calls=%fused_computation.134 | custom fusion | flops 2048 | bytes 131076 | tf_op jit(solution)/shard_map/scatter-add | solution.py:131
  18.0 4.3 reduce_sum.144
  22.2 4.8 copy.51
  27.1 7.2 %fusion.188 = (f32[16,8,1024,1]{0,1,3,2:T(8,128)}, f32[16,8,1024,1]{0,1,3,2:T(8,128)}) fusion(f32[16,8,1024,2]{0,1,3,2:T(8,128)} %bitcast.153), kind=kLoop, calls=%fused_computation.222 | loop fusion | bytes 2097152 | tf_op jit(solution)/shard_map/slice | solution.py:89
  40.3 4.0 fusion.14
  44.3 4.4 collective-permute-start
  51.0 10.6 %select_add_fusion = f32[8,24]{1,0:T(8,128)S(1)} fusion(f32[]{:T(128)} %bitcast.25, f32[]{:T(128)} %bitcast.24, f32[]{:T(128)} %bitcast.23, f32[]{:T(128)} %bitcast.22, f32[]{:T(128)} %bitcast.21, f32[]{:T(128)} %bitcast.20, f32[]{:T(128)} %bitcast.19, f32[]{:T(128)} %bitcast.18, f32[]{:T(128)} %bitcast.17, f32[]{:T(128)} %bitcast.16, f32[]{:T(128)} %bitcast.15, ...), kind=kLoop, calls=%fused_computation.170 | loop fusion | flops 9792 | bytes 836 | tf_op jit(solution)/shard_map/add | solution.py:75
  63.2 5.4 collective-permute-start.2
  70.0 7.2 %collective-permute-done.2 = f32[16,8,1024]{2,1,0:T(8,128)S(1)} collective-permute-done((f32[16,8,1024]{2,1,0:T(8,128)S(1)}, f32[16,8,1024]{2,1,0:T(8,128)S(1)}, u32[]{:S(2)}, u32[]{:S(2)}) %collective-permute-start.2) | collective-permute-done | bytes 524320 | tf_op jit(solution)/shard_map/ppermute | solution.py:22
  77.2 6.7 %collective-permute-done.3 = f32[16,8,1024]{2,1,0:T(8,128)S(1)} collective-permute-done((f32[16,8,1024]{2,1,0:T(8,128)S(1)}, f32[16,8,1024]{2,1,0:T(8,128)S(1)}, u32[]{:S(2)}, u32[]{:S(2)}) %collective-permute-start.3) | collective-permute-done | bytes 524320 | tf_op jit(solution)/shard_map/ppermute | solution.py:25
  84.8 3.9 fusion.12
  89.2 6.2 %copy.54 = f32[16,8,1024,2]{0,1,3,2:T(8,128)} copy(f32[16,8,1024,2]{2,1,0,3:T(8,128)S(1)} %pad_maximum_fusion) | data formatting | bytes 2097152 | tf_op jit(solution)/shard_map/stack | solution.py:81
  95.4 5.4 copy.55
  103.3 3.7 reshape.218
  108.9 16.6 %gather_fusion = f32[2048]{0:T(1024)S(1)} fusion(f32[16,2048]{1,0:T(8,128)S(1)} %broadcast_multiply_fusion.2, s32[2048]{0:T(1024)S(1)} %bitcast.147), kind=kCustom, calls=%fused_computation | custom fusion | bytes 32768 | tf_op jit(solution)/shard_map/gather | solution.py:154
  126.3 7.8 %all-to-all-start = ((f32[16,1,2048]{2,1,0:T(1,128)}), f32[16,1,2048]{2,1,0:T(1,128)S(1)}, u32[]{:S(2)}, u32[]{:S(2)}) async-start(f32[16,1,2048]{2,1,0:T(1,128)} %broadcast_in_dim.145), calls=%async_computation | async-start | bytes 262144 | tf_op jit(solution)/shard_map/all_to_all | solution.py:32
  134.1 6.1 %all-to-all-done = f32[16,1,2048]{2,1,0:T(1,128)S(1)} async-done(((f32[16,1,2048]{2,1,0:T(1,128)}), f32[16,1,2048]{2,1,0:T(1,128)S(1)}, u32[]{:S(2)}, u32[]{:S(2)}) %all-to-all-start) | async-done | bytes 131104 | tf_op jit(solution)/shard_map/all_to_all | solution.py:32
  141.0 4.5 all-reduce.14
  145.4 8.0 %all-reduce.5 = (f32[]{:T(128)}, f32[]{:T(128)}) all-reduce(f32[]{:T(128)} %get-tuple-element.30, f32[]{:T(128)} %get-tuple-element.31), channel_id=1, replica_groups=mesh['mem_0'=2,'mem_1'=4,'mem_2'=2,'lat_0'=2,'lat_1'=16] {'mem_1'}, use_global_device_ids=true, to_apply=%region_4.5 | all-reduce | flops 2 | bytes 16 | tf_op jit(solution)/shard_map/psum | solution.py:42
  153.4 6.0 %all-reduce.11 = (f32[]{:T(128)}, f32[]{:T(128)}) all-reduce(f32[]{:T(128)} %get-tuple-element.12, f32[]{:T(128)} %get-tuple-element.13), channel_id=1, replica_groups=mesh['mem_0'=2,'mem_1'=4,'mem_2'=2,'lat_0'=2,'lat_1'=16] {'mem_2'}, use_global_device_ids=true, to_apply=%region_5.6 | all-reduce | flops 2 | bytes 16 | tf_op jit(solution)/shard_map/psum | solution.py:42
  159.5 12.3 %all-reduce.8 = (f32[]{:T(128)}, f32[]{:T(128)}) all-reduce(f32[]{:T(128)} %get-tuple-element.24, f32[]{:T(128)} %get-tuple-element.25), channel_id=1, replica_groups=mesh['mem_0'=2,'mem_1'=4,'mem_2'=2,'lat_0'=2,'lat_1'=16] {'lat_0'}, use_global_device_ids=true, to_apply=%region_6.7 | all-reduce | flops 2 | bytes 16 | tf_op jit(solution)/shard_map/psum | solution.py:42
  171.7 26.9 %all-reduce.2 = (f32[]{:T(128)}, f32[]{:T(128)}) all-reduce(f32[]{:T(128)} %get-tuple-element.18, f32[]{:T(128)} %get-tuple-element.19), channel_id=1, replica_groups=mesh['mem_0'=2,'mem_1'=4,'mem_2'=2,'lat_0'=2,'lat_1'=16] {'lat_1'}, use_global_device_ids=true, to_apply=%region_7.8 | all-reduce | flops 2 | bytes 16 | tf_op jit(solution)/shard_map/psum | solution.py:42
  200.6 11.3 %scatter_custom_fusion.1 = f32[32768]{0:T(1024)S(1)} fusion(s32[2048]{0:T(1024)S(1)} %bitcast.176, f32[2048]{0:T(1024)S(1)} %multiply_select_fusion.1, f32[]{:T(128)} %constant.35.clone.1), kind=kCustom, calls=%fused_computation.132 | custom fusion | flops 2048 | bytes 131076 | tf_op jit(solution)/shard_map/scatter-add | solution.py:131
  217.1 4.3 reduce_sum.149
  221.4 4.8 copy.57
  226.2 7.2 %fusion.187 = (f32[16,8,1024,1]{0,1,3,2:T(8,128)}, f32[16,8,1024,1]{0,1,3,2:T(8,128)}) fusion(f32[16,8,1024,2]{0,1,3,2:T(8,128)} %bitcast.154), kind=kLoop, calls=%fused_computation.221 | loop fusion | bytes 2097152 | tf_op jit(solution)/shard_map/slice | solution.py:89
  239.4 4.0 fusion.10
  246.2 4.6 collective-permute-done.4
  250.8 3.8 collective-permute-done.5
  260.4 4.8 collective-permute-done.6
  265.2 4.1 collective-permute-done.7
  270.2 3.9 fusion.8
  274.6 6.2 %copy.60 = f32[16,8,1024,2]{0,1,3,2:T(8,128)} copy(f32[16,8,1024,2]{2,1,0,3:T(8,128)S(1)} %pad_maximum_fusion.1) | data formatting | bytes 2097152 | tf_op jit(solution)/shard_map/stack | solution.py:81
  280.8 5.4 copy.61
  288.7 3.7 reshape.222
  294.3 16.6 %gather_fusion.1 = f32[2048]{0:T(1024)S(1)} fusion(f32[16,2048]{1,0:T(8,128)S(1)} %broadcast_multiply_fusion.1, s32[2048]{0:T(1024)S(1)} %bitcast.148), kind=kCustom, calls=%fused_computation.1 | custom fusion | bytes 32768 | tf_op jit(solution)/shard_map/gather | solution.py:154
  311.0 19.6 %all_to_all.23 = f32[16,1,2048]{2,1,0:T(1,128)S(1)} all-to-all(f32[16,1,2048]{2,1,0:T(1,128)S(1)} %broadcast_in_dim.147), channel_id=1, replica_groups=mesh['mem_0'=2,'mem_1'=4,'mem_2'=2,'lat_0'=2,'lat_1'=16] {'mem_0','mem_1..., dimensions={0} | all-to-all | bytes 262144 | tf_op jit(solution)/shard_map/all_to_all | solution.py:32
  331.4 4.5 all-reduce.13
  335.9 8.0 %all-reduce.4 = (f32[]{:T(128)}, f32[]{:T(128)}) all-reduce(f32[]{:T(128)} %get-tuple-element.28, f32[]{:T(128)} %get-tuple-element.29), channel_id=1, replica_groups=mesh['mem_0'=2,'mem_1'=4,'mem_2'=2,'lat_0'=2,'lat_1'=16] {'mem_1'}, use_global_device_ids=true, to_apply=%region_20.21 | all-reduce | flops 2 | bytes 16 | tf_op jit(solution)/shard_map/psum | solution.py:42
  343.8 6.0 %all-reduce.10 = (f32[]{:T(128)}, f32[]{:T(128)}) all-reduce(f32[]{:T(128)} %get-tuple-element.10, f32[]{:T(128)} %get-tuple-element.11), channel_id=1, replica_groups=mesh['mem_0'=2,'mem_1'=4,'mem_2'=2,'lat_0'=2,'lat_1'=16] {'mem_2'}, use_global_device_ids=true, to_apply=%region_21.22 | all-reduce | flops 2 | bytes 16 | tf_op jit(solution)/shard_map/psum | solution.py:42
  349.8 8.7 %all-reduce.7 = (f32[]{:T(128)}, f32[]{:T(128)}) all-reduce(f32[]{:T(128)} %get-tuple-element.22, f32[]{:T(128)} %get-tuple-element.23), channel_id=1, replica_groups=mesh['mem_0'=2,'mem_1'=4,'mem_2'=2,'lat_0'=2,'lat_1'=16] {'lat_0'}, use_global_device_ids=true, to_apply=%region_22.23 | all-reduce | flops 2 | bytes 16 | tf_op jit(solution)/shard_map/psum | solution.py:42
  358.5 27.2 %all-reduce.1 = (f32[]{:T(128)}, f32[]{:T(128)}) all-reduce(f32[]{:T(128)} %get-tuple-element.16, f32[]{:T(128)} %get-tuple-element.17), channel_id=1, replica_groups=mesh['mem_0'=2,'mem_1'=4,'mem_2'=2,'lat_0'=2,'lat_1'=16] {'lat_1'}, use_global_device_ids=true, to_apply=%region_23.24 | all-reduce | flops 2 | bytes 16 | tf_op jit(solution)/shard_map/psum | solution.py:42
  388.3 11.4 %scatter_custom_fusion.2 = f32[32768]{0:T(1024)S(1)} fusion(s32[2048]{0:T(1024)} %bitcast.177, f32[2048]{0:T(1024)S(1)} %get-tuple-element.32, f32[]{:T(128)} %constant.35.clone.1), kind=kCustom, calls=%fused_computation.130 | custom fusion | flops 2048 | bytes 131584 | tf_op jit(solution)/shard_map/scatter-add | solution.py:131
  404.9 4.3 reduce_sum.154
  409.2 4.8 copy.63
  414.0 7.2 %fusion.186 = (f32[16,8,1024,1]{0,1,3,2:T(8,128)}, f32[16,8,1024,1]{0,1,3,2:T(8,128)}) fusion(f32[16,8,1024,2]{0,1,3,2:T(8,128)} %bitcast.155), kind=kLoop, calls=%fused_computation.220 | loop fusion | bytes 2097152 | tf_op jit(solution)/shard_map/slice | solution.py:89
  427.8 5.1 fusion.6
  435.8 4.5 collective-permute-done.8
  440.3 3.8 collective-permute-done.9
  450.6 4.8 collective-permute-done.10
  455.4 3.8 collective-permute-done.11
  460.2 3.9 fusion.4
  464.5 6.2 %copy.66 = f32[16,8,1024,2]{0,1,3,2:T(8,128)} copy(f32[16,8,1024,2]{2,1,0,3:T(8,128)S(1)} %pad_maximum_fusion.2) | data formatting | bytes 2097152 | tf_op jit(solution)/shard_map/stack | solution.py:81
  470.7 5.4 copy.67
  484.2 16.6 %gather_fusion.2 = f32[2048]{0:T(1024)S(1)} fusion(f32[16,2048]{1,0:T(8,128)S(1)} %broadcast_multiply_fusion, s32[2048]{0:T(1024)S(1)} %bitcast.149), kind=kCustom, calls=%fused_computation.2 | custom fusion | bytes 32768 | tf_op jit(solution)/shard_map/gather | solution.py:154
  501.6 14.7 %all-to-all-start.2 = ((f32[16,1,2048]{2,1,0:T(1,128)}), f32[16,1,2048]{2,1,0:T(1,128)S(1)}, u32[]{:S(2)}, u32[]{:S(2)}) async-start(f32[16,1,2048]{2,1,0:T(1,128)} %broadcast_in_dim.149), calls=%async_computation.2 | async-start | bytes 262144 | tf_op jit(solution)/shard_map/all_to_all | solution.py:32
  516.3 6.2 %all-to-all-done.2 = f32[16,1,2048]{2,1,0:T(1,128)S(1)} async-done(((f32[16,1,2048]{2,1,0:T(1,128)}), f32[16,1,2048]{2,1,0:T(1,128)S(1)}, u32[]{:S(2)}, u32[]{:S(2)}) %all-to-all-start.2) | async-done | bytes 131104 | tf_op jit(solution)/shard_map/all_to_all | solution.py:32
  523.1 4.4 all-reduce.12
  527.5 8.0 %all-reduce.3 = (f32[]{:T(128)}, f32[]{:T(128)}) all-reduce(f32[]{:T(128)} %get-tuple-element.26, f32[]{:T(128)} %get-tuple-element.27), channel_id=1, replica_groups=mesh['mem_0'=2,'mem_1'=4,'mem_2'=2,'lat_0'=2,'lat_1'=16] {'mem_1'}, use_global_device_ids=true, to_apply=%region_36.37 | all-reduce | flops 2 | bytes 16 | tf_op jit(solution)/shard_map/psum | solution.py:42
  535.6 5.9 all-reduce.9
  541.5 8.6 %all-reduce.6 = (f32[]{:T(128)}, f32[]{:T(128)}) all-reduce(f32[]{:T(128)} %get-tuple-element.20, f32[]{:T(128)} %get-tuple-element.21), channel_id=1, replica_groups=mesh['mem_0'=2,'mem_1'=4,'mem_2'=2,'lat_0'=2,'lat_1'=16] {'lat_0'}, use_global_device_ids=true, to_apply=%region_38.39 | all-reduce | flops 2 | bytes 16 | tf_op jit(solution)/shard_map/psum | solution.py:42
  550.2 27.0 %all-reduce = (f32[]{:T(128)}, f32[]{:T(128)}) all-reduce(f32[]{:T(128)} %get-tuple-element.14, f32[]{:T(128)} %get-tuple-element.15), channel_id=1, replica_groups=mesh['mem_0'=2,'mem_1'=4,'mem_2'=2,'lat_0'=2,'lat_1'=16] {'lat_1'}, use_global_device_ids=true, to_apply=%region_39.40 | all-reduce | flops 2 | bytes 16 | tf_op jit(solution)/shard_map/psum | solution.py:42
  579.7 11.8 %all-to-all-start.3 = ((f32[16,16,128]{2,1,0:T(8,128)}), f32[16,16,128]{2,1,0:T(8,128)S(1)}, u32[]{:S(2)}, u32[]{:S(2)}) async-start(f32[16,16,128]{2,1,0:T(8,128)} %bitcast_bitcast_fusion), calls=%async_computation.3 | async-start | bytes 262144 | tf_op jit(solution)/shard_map/all_to_all | solution.py:52
  592.4 5.2 all-to-all-done.3
  (99 shorter events, 84.6 us)
Async XLA Ops:
  2.1 198.6 %copy-start.10 = (s32[2048,1]{0,1:T(1,128)}, s32[2048,1]{0,1:T(1,128)S(1)}, u32[]{:S(2)}) copy-start(s32[2048,1]{0,1:T(1,128)S(1)} %get-tuple-element.47) | copy-start | bytes 24580
  44.3 17.3 %collective-permute-start = (f32[16,8,1024]{2,1,0:T(8,128)S(1)}, f32[16,8,1024]{2,1,0:T(8,128)S(1)}, u32[]{:S(2)}, u32[]{:S(2)}) collective-permute-start(f32[16,8,1024]{2,1,0:T(8,128)S(1)} %fusion.14), channel_id=1, source_target_pairs={{0,1},{1,2},{2,3},{3,4},{4,5},{5,6},{6,7},{7,8},{8,9},{9,10},{10,1... | collective-permute-start | bytes 1572872 | tf_op jit(solution)/shard_map/ppermute | solution.py:22
  48.7 12.9 %collective-permute-start.1 = (f32[16,8,1024]{2,1,0:T(8,128)S(1)}, f32[16,8,1024]{2,1,0:T(8,128)S(1)}, u32[]{:S(2)}, u32[]{:S(2)}) collective-permute-start(f32[16,8,1024]{2,1,0:T(8,128)S(1)} %fusion.14), channel_id=1, source_target_pairs={{1,0},{2,1},{3,2},{4,3},{5,4},{6,5},{7,6},{8,7},{9,8},{10,9},{11,1... | collective-permute-start | bytes 1572872 | tf_op jit(solution)/shard_map/ppermute | solution.py:25
  61.6 207.7 %copy-start.7 = (f32[8,24]{1,0:T(8,128)}, f32[8,24]{1,0:T(8,128)S(1)}, u32[]{:S(2)}) copy-start(f32[8,24]{1,0:T(8,128)S(1)} %select_add_fusion) | copy-start | bytes 2308
  63.2 13.9 %collective-permute-start.2 = (f32[16,8,1024]{2,1,0:T(8,128)S(1)}, f32[16,8,1024]{2,1,0:T(8,128)S(1)}, u32[]{:S(2)}, u32[]{:S(2)}) collective-permute-start(f32[16,8,1024]{2,1,0:T(8,128)S(1)} %get-tuple-element.45), channel_id=1, source_target_pairs={{0,1},{1,2},{2,3},{3,4},{4,5},{5,6},{6,7},{7,8},{8,9},{9,10},{10,1... | collective-permute-start | bytes 1572872 | tf_op jit(solution)/shard_map/ppermute | solution.py:22
  68.7 15.2 %collective-permute-start.3 = (f32[16,8,1024]{2,1,0:T(8,128)S(1)}, f32[16,8,1024]{2,1,0:T(8,128)S(1)}, u32[]{:S(2)}, u32[]{:S(2)}) collective-permute-start(f32[16,8,1024]{2,1,0:T(8,128)S(1)} %get-tuple-element.45), channel_id=1, source_target_pairs={{1,0},{2,1},{3,2},{4,3},{5,4},{6,5},{7,6},{8,7},{9,8},{10,9},{11,1... | collective-permute-start | bytes 1572872 | tf_op jit(solution)/shard_map/ppermute | solution.py:25
  100.8 6.2 %copy-start = (bf16[16,16,2048]{2,1,0:T(8,128)(2,1)S(1)}, bf16[16,16,2048]{2,1,0:T(8,128)(2,1)}, u32[]{:S(2)}) copy-start(bf16[16,16,2048]{2,1,0:T(8,128)(2,1)} %param.5) | copy-start | bytes 3145732
  108.9 31.4 %copy-start.2 = (f32[1,2048]{1,0:T(1,128)S(1)}, f32[1,2048]{1,0:T(1,128)}, u32[]{:S(2)}) copy-start(f32[1,2048]{1,0:T(1,128)} %param.9) | copy-start | bytes 24580
  108.9 31.4 %copy-start.3 = (f32[1,2048]{1,0:T(1,128)S(1)}, f32[1,2048]{1,0:T(1,128)}, u32[]{:S(2)}) copy-start(f32[1,2048]{1,0:T(1,128)} %param.8) | copy-start | bytes 24580
  126.3 13.9 %all-to-all-start = ((f32[16,1,2048]{2,1,0:T(1,128)}), f32[16,1,2048]{2,1,0:T(1,128)S(1)}, u32[]{:S(2)}, u32[]{:S(2)}) async-start(f32[16,1,2048]{2,1,0:T(1,128)} %broadcast_in_dim.145), calls=%async_computation | async-start | bytes 262144 | tf_op jit(solution)/shard_map/all_to_all | solution.py:32
  140.2 81.1 %copy-start.5 = (f32[2048]{0:T(1024)}, f32[2048]{0:T(1024)S(1)}, u32[]{:S(2)}) copy-start(f32[2048]{0:T(1024)S(1)} %reduce_sum.147) | copy-start | bytes 24580
  243.4 7.4 %collective-permute-start.4 = (f32[16,8,1024]{2,1,0:T(8,128)S(1)}, f32[16,8,1024]{2,1,0:T(8,128)S(1)}, u32[]{:S(2)}, u32[]{:S(2)}) collective-permute-start(f32[16,8,1024]{2,1,0:T(8,128)S(1)} %fusion.10), channel_id=1, source_target_pairs={{0,1},{1,2},{2,3},{3,4},{4,5},{5,6},{6,7},{7,8},{8,9},{9,10},{10,1... | collective-permute-start | bytes 1572872 | tf_op jit(solution)/shard_map/ppermute | solution.py:22
  244.8 9.9 %collective-permute-start.5 = (f32[16,8,1024]{2,1,0:T(8,128)S(1)}, f32[16,8,1024]{2,1,0:T(8,128)S(1)}, u32[]{:S(2)}, u32[]{:S(2)}) collective-permute-start(f32[16,8,1024]{2,1,0:T(8,128)S(1)} %fusion.10), channel_id=1, source_target_pairs={{1,0},{2,1},{3,2},{4,3},{5,4},{6,5},{7,6},{8,7},{9,8},{10,9},{11,1... | collective-permute-start | bytes 1572872 | tf_op jit(solution)/shard_map/ppermute | solution.py:25
  256.3 8.9 %collective-permute-start.6 = (f32[16,8,1024]{2,1,0:T(8,128)S(1)}, f32[16,8,1024]{2,1,0:T(8,128)S(1)}, u32[]{:S(2)}, u32[]{:S(2)}) collective-permute-start(f32[16,8,1024]{2,1,0:T(8,128)S(1)} %get-tuple-element.43), channel_id=1, source_target_pairs={{0,1},{1,2},{2,3},{3,4},{4,5},{5,6},{6,7},{7,8},{8,9},{9,10},{10,1... | collective-permute-start | bytes 1572872 | tf_op jit(solution)/shard_map/ppermute | solution.py:22
  259.1 10.2 %collective-permute-start.7 = (f32[16,8,1024]{2,1,0:T(8,128)S(1)}, f32[16,8,1024]{2,1,0:T(8,128)S(1)}, u32[]{:S(2)}, u32[]{:S(2)}) collective-permute-start(f32[16,8,1024]{2,1,0:T(8,128)S(1)} %get-tuple-element.43), channel_id=1, source_target_pairs={{1,0},{2,1},{3,2},{4,3},{5,4},{6,5},{7,6},{8,7},{9,8},{10,9},{11,1... | collective-permute-start | bytes 1572872 | tf_op jit(solution)/shard_map/ppermute | solution.py:25
  294.2 36.5 %copy-start.4 = (f32[1,2048]{1,0:T(1,128)S(1)}, f32[1,2048]{1,0:T(1,128)}, u32[]{:S(2)}) copy-start(f32[1,2048]{1,0:T(1,128)} %param.8) | copy-start | bytes 24580
  294.3 36.5 %copy-start.6 = (f32[2048]{0:T(1024)S(1)}, f32[2048]{0:T(1024)}, u32[]{:S(2)}) copy-start(f32[2048]{0:T(1024)} %copy-done.5) | copy-start | bytes 24580
  427.8 16.3 %copy-start.8 = (f32[8,24]{1,0:T(8,128)S(1)}, f32[8,24]{1,0:T(8,128)}, u32[]{:S(2)}) copy-start(f32[8,24]{1,0:T(8,128)} %copy-done.7) | copy-start | bytes 2308
  432.9 7.4 %collective-permute-start.8 = (f32[16,8,1024]{2,1,0:T(8,128)S(1)}, f32[16,8,1024]{2,1,0:T(8,128)S(1)}, u32[]{:S(2)}, u32[]{:S(2)}) collective-permute-start(f32[16,8,1024]{2,1,0:T(8,128)S(1)} %fusion.6), channel_id=1, source_target_pairs={{0,1},{1,2},{2,3},{3,4},{4,5},{5,6},{6,7},{7,8},{8,9},{9,10},{10,1... | collective-permute-start | bytes 1572872 | tf_op jit(solution)/shard_map/ppermute | solution.py:22
  434.2 9.9 %collective-permute-start.9 = (f32[16,8,1024]{2,1,0:T(8,128)S(1)}, f32[16,8,1024]{2,1,0:T(8,128)S(1)}, u32[]{:S(2)}, u32[]{:S(2)}) collective-permute-start(f32[16,8,1024]{2,1,0:T(8,128)S(1)} %fusion.6), channel_id=1, source_target_pairs={{1,0},{2,1},{3,2},{4,3},{5,4},{6,5},{7,6},{8,7},{9,8},{10,9},{11,1... | collective-permute-start | bytes 1572872 | tf_op jit(solution)/shard_map/ppermute | solution.py:25
  446.6 8.8 %collective-permute-start.10 = (f32[16,8,1024]{2,1,0:T(8,128)S(1)}, f32[16,8,1024]{2,1,0:T(8,128)S(1)}, u32[]{:S(2)}, u32[]{:S(2)}) collective-permute-start(f32[16,8,1024]{2,1,0:T(8,128)S(1)} %get-tuple-element.40), channel_id=1, source_target_pairs={{0,1},{1,2},{2,3},{3,4},{4,5},{5,6},{6,7},{7,8},{8,9},{9,10},{10,1... | collective-permute-start | bytes 1572872 | tf_op jit(solution)/shard_map/ppermute | solution.py:22
  449.3 9.9 %collective-permute-start.11 = (f32[16,8,1024]{2,1,0:T(8,128)S(1)}, f32[16,8,1024]{2,1,0:T(8,128)S(1)}, u32[]{:S(2)}, u32[]{:S(2)}) collective-permute-start(f32[16,8,1024]{2,1,0:T(8,128)S(1)} %get-tuple-element.40), channel_id=1, source_target_pairs={{1,0},{2,1},{3,2},{4,3},{5,4},{6,5},{7,6},{8,7},{9,8},{10,9},{11,1... | collective-permute-start | bytes 1572872 | tf_op jit(solution)/shard_map/ppermute | solution.py:25
  484.2 38.3 %copy-start.9 = (f32[2048]{0:T(1024)S(1)}, f32[2048]{0:T(1024)}, u32[]{:S(2)}) copy-start(f32[2048]{0:T(1024)} %get-tuple-element.33) | copy-start | bytes 24580
  484.2 107.3 %copy-start.1 = (f32[16,8,1024]{2,1,0:T(8,128)S(1)}, f32[16,8,1024]{2,1,0:T(8,128)}, u32[]{:S(2)}) copy-start(f32[16,8,1024]{2,1,0:T(8,128)} %get-tuple-element.66) | copy-start | bytes 1572868
  501.6 20.8 %all-to-all-start.2 = ((f32[16,1,2048]{2,1,0:T(1,128)}), f32[16,1,2048]{2,1,0:T(1,128)S(1)}, u32[]{:S(2)}, u32[]{:S(2)}) async-start(f32[16,1,2048]{2,1,0:T(1,128)} %broadcast_in_dim.149), calls=%async_computation.2 | async-start | bytes 262144 | tf_op jit(solution)/shard_map/all_to_all | solution.py:32
  579.7 18.0 %all-to-all-start.3 = ((f32[16,16,128]{2,1,0:T(8,128)}), f32[16,16,128]{2,1,0:T(8,128)S(1)}, u32[]{:S(2)}, u32[]{:S(2)}) async-start(f32[16,16,128]{2,1,0:T(8,128)} %bitcast_bitcast_fusion), calls=%async_computation.3 | async-start | bytes 262144 | tf_op jit(solution)/shard_map/all_to_all | solution.py:52
where the time goes:
time: 609 us; the launch traced here: 599 us
  blocking collectives  186 us (31%)
  local copies, waits for them, and re-layouts  170 us (28%)
  other arithmetic  75.7 us (12%)
  waiting for transfers between devices  65.8 us (11%)
  starting transfers between devices  60.7 us (10%)
  matrix products  32.5 us (5%)
  between operations  8.29 us (1%)
    psum x15, blocking collectives, one_axis_at_a_time(): return functools.reduce(lax.psum, axes, value)  166 us
    gather x3, local copies, waits for them, and re-layouts, on_device(): hits = over_copies(partial_image[row_index, col_index], MEM)  50 us
    scatter-add x3, other arithmetic, on_device(): obs_field = jnp.zeros((fine_rows * lon_cells,), jnp.float32).at[obs_index...  34 us
    ppermute x6, waiting for transfers between devices, padded_2(): lax.ppermute(lax.slice_in_dim(block, block.shape[dim] - width, None, axis...  25.9 us
    all_to_all x2, starting transfers between devices, sent_to_all(): lax.all_to_all(jnp.broadcast_to(value[None], (devices, *value.shape)), ax...  22.5 us
    ppermute x6, waiting for transfers between devices, padded_2(): lax.ppermute(lax.slice_in_dim(block, 0, width, axis=dim), axis, backward)  22.4 us
    slice x3, local copies, waits for them, and re-layouts, narrow_lon(): paired[..., 0] + 0.5 * odd_part + 0.5 * jnp.roll(odd_part, 1, axis=-1)  21.6 us
    all_to_all x1, blocking collectives, sent_to_all(): lax.all_to_all(jnp.broadcast_to(value[None], (devices, *value.shape)), ax...  19.6 us
  transfers between devices with their start and end apart: 15, of which 13 were waited for; matrix products, arithmetic and copies ran while one was open for 2% of the time, Pallas kernels for 0%

commit v1 on v0

v1 whole, which is shorter than its diff:
```python
import functools

import jax
import jax.numpy as jnp
import ml_dtypes
import numpy as np
from jax import lax
from jax.experimental import pallas as pl
from jax.experimental.pallas import tpu as pltpu
from jax.sharding import PartitionSpec as P

HALO = 8
LSIG = 3
ITERS = 3
NEAR = 5
BLOCK = 256
PAD = 128
F32 = jnp.float32
BF16 = jnp.bfloat16
MESH = pl.DeviceIdType.MESH


def window_matrices(coarse_cols):
    columns = np.arange(coarse_cols)
    distance = np.minimum(columns, coarse_cols - columns).astype(np.float32)
    first = np.exp(-distance * distance / np.float32(2.0 * LSIG * LSIG)).astype(np.float64)
    circulant = first[np.abs(columns[:, None] - columns[None, :])]
    squared = first @ circulant
    apart = np.arange(BLOCK + 2 * PAD)[:, None] - PAD - np.arange(BLOCK)[None, :]
    parts = []
    for row in (first, squared):
        inside = np.abs(apart) < min(PAD, coarse_cols // 2)
        window = np.where(inside, row[np.abs(apart) % coarse_cols], 0.0).astype(np.float32)
        high = window.astype(ml_dtypes.bfloat16)
        parts += [high, (window - high.astype(np.float32)).astype(ml_dtypes.bfloat16)]
    return np.stack(parts)


def widen_matrix():
    fine = np.arange(256) * 0.5
    coarse = np.arange(256)
    return np.maximum(0.0, 1.0 - np.abs(coarse[:, None] - fine[None, :])).astype(
        ml_dtypes.bfloat16
    )


def split_rows_matrix(members, rows):
    matrix = np.zeros((members * rows, members * rows), ml_dtypes.bfloat16)
    for member in range(members):
        for row in range(rows):
            to = (row % 2) * members * (rows // 2) + member * (rows // 2) + row // 2
            matrix[to, member * rows + row] = 1.0
    return matrix


def halves(value):
    high = value.astype(BF16)
    return high, (value - high.astype(F32)).astype(BF16)


def dot(a, b):
    return jnp.dot(a, b, preferred_element_type=F32)


def body(
    n_mem,
    n_lat,
    cells_ref,
    count_ref,
    innov_ref,
    scale_ref,
    pert_ref,
    sel_ref,
    win_ref,
    widen_ref,
    control_ref,
    inc_ref,
    meta,
    bvals,
    spread,
    chosen,
    picked,
    onehot,
    filt,
    filt2,
    target,
    scale,
    live,
    observed,
    summed,
    q_now,
    weight,
    acc,
    vext,
    vwide,
    along,
    image,
    image_acc,
    hsend,
    hrecv,
    hnear,
    ssend,
    srecv,
    irecv,
    meta_send,
    meta_recv,
    b_send,
    b_recv,
    h_send,
    h_recv,
    n_send,
    n_recv,
    s_send,
    s_recv,
    i_send,
    i_recv,
):
    members, fine_rows, fine_cols = pert_ref.shape
    rows, cols = fine_rows // 2, fine_cols // 2
    slots = cells_ref.shape[1]
    flat = members * rows
    c = float((members * n_mem - 1) ** -0.5)
    mem = lax.axis_index("mem")
    lat = lax.axis_index("lat")
    barrier = pltpu.get_barrier_semaphore()

    def mem_peer(r):
        return {"mem": lax.rem(mem + r, n_mem)}

    def lat_peer(r):
        return {"lat": lax.rem(lat + r, n_lat)}

    def offset(n):
        return ((n + 1) // 2) * (1 - 2 * (n % 2))

    def remote(src, dst, send, recv, device):
        return pltpu.make_async_remote_copy(
            src_ref=src,
            dst_ref=dst,
            send_sem=send,
            recv_sem=recv,
            device_id=device,
            device_id_type=MESH,
        )

    def wait_all(ref, sem):
        pltpu.make_async_copy(ref, ref, sem).wait()

    @pl.loop(1, n_mem)
    def _(r):
        pl.semaphore_signal(barrier, inc=1, device_id=mem_peer(r), device_id_type=MESH)

    @pl.loop(1, n_lat)
    def _(r):
        pl.semaphore_signal(barrier, inc=1, device_id=lat_peer(r), device_id_type=MESH)

    cells = cells_ref[...]
    row = cells >> (fine_cols.bit_length() - 1)
    col = cells & (fine_cols - 1)
    coarse_row = (row >> 1).astype(F32)
    slot_id = lax.broadcasted_iota(jnp.int32, (1, slots), 1)
    meta[0, 0:1, :] = col.astype(F32) * 0.5
    meta[0, 1:2, :] = coarse_row
    meta[0, 2:3, :] = innov_ref[...]
    meta[0, 3:4, :] = scale_ref[...]
    meta[0, 4:5, :] = jnp.where(slot_id < count_ref[0], 1.0, 0.0)
    meta[0, 5:6, :] = col.astype(F32)
    meta[0, 6:7, :] = (row & 1).astype(F32)
    meta[0, 7:8, :] = jnp.zeros((1, slots), F32)
    pl.semaphore_wait(barrier, n_mem + n_lat - 2)

    def near_peer(n):
        return {"lat": lax.rem(lat - offset(n) + n_lat, n_lat)}

    def meta_copy(n):
        return remote(
            meta.at[0], meta.at[n], meta_send.at[n - 1], meta_recv.at[n - 1], near_peer(n)
        )

    def value_copy(n):
        return remote(
            bvals.at[0], bvals.at[n], b_send.at[n - 1], b_recv.at[n - 1], near_peer(n)
        )

    @pl.loop(1, NEAR)
    def _(n):
        meta_copy(n).start()

    @pl.loop(0, fine_cols // BLOCK)
    def _(j):
        at = pl.ds(pl.multiple_of(j * BLOCK, BLOCK), BLOCK)
        picked[:, at] = dot(
            sel_ref[...], pert_ref[:, :, at].reshape(members * fine_rows, BLOCK)
        ).astype(BF16)

    @pl.loop(0, slots // BLOCK)
    def _(j):
        at = pl.ds(pl.multiple_of(j * BLOCK, BLOCK), BLOCK)
        column = meta[0, 5:6, at]
        place = lax.broadcasted_iota(jnp.int32, (fine_cols, BLOCK), 0).astype(F32)
        hit = jnp.where(place == column, 1.0, 0.0).astype(BF16)
        both = dot(picked[...], hit)
        value = jnp.where(meta[0, 6:7, at] > 0.5, both[flat:], both[:flat])
        own = lax.broadcasted_iota(jnp.int32, (rows, BLOCK), 0).astype(F32) == meta[0, 1:2, at]
        value = jnp.where(own[None], value.reshape(members, rows, BLOCK), 0.0)
        chosen[:, at] = value.reshape(flat, BLOCK).astype(BF16)
        bvals[0, :, at] = jnp.sum(value, axis=1)

    @pl.loop(1, NEAR)
    def _(n):
        value_copy(n).start()

    target[...] = jnp.zeros_like(target)
    scale[...] = jnp.ones_like(scale)
    live[...] = jnp.zeros_like(live)
    observed[...] = jnp.zeros_like(observed)
    summed[...] = jnp.zeros_like(summed)

    @pl.loop(0, NEAR)
    def _(n):
        @pl.when(n > 0)
        def _():
            meta_copy(n).wait_recv()

        x = meta[n, 0:1, :]
        step = 128

        @pl.loop(0, cols // step)
        def _(j):
            start = pl.multiple_of(j * step, step)
            place = (lax.broadcasted_iota(jnp.int32, (step, slots), 0) + start).astype(F32)
            hat = jnp.maximum(1.0 - jnp.abs(x - place), 0.0)
            onehot[n, pl.ds(start, step), :] = hat.astype(BF16)

        place = lax.broadcasted_iota(jnp.int32, (16, slots), 0).astype(F32)
        hat = jnp.maximum(
            jnp.maximum(1.0 - jnp.abs(x - place), 1.0 - jnp.abs(x - (place + float(cols)))), 0.0
        )
        onehot[n, 0:16, :] = hat.astype(BF16)

        reach = rows + 2 * HALO
        between = lax.broadcasted_iota(jnp.int32, (reach, slots), 0) - HALO
        whole = between + lat * rows
        there = meta[n, 1:2, :] + (offset(n) * rows).astype(F32)
        apart = between.astype(F32) - there
        spread_sq = 2.0 * (HALO / 2.0) ** 2
        taps = jnp.where(
            (jnp.abs(apart) <= HALO) & (whole >= 0) & (whole < n_lat * rows),
            (0.5 * c) * jnp.exp(-apart * apart / spread_sq),
            0.0,
        )
        filt[n] = taps[HALO : HALO + rows]
        own = lax.broadcasted_iota(jnp.int32, (rows, reach), 0).astype(F32)
        middle = lax.broadcasted_iota(jnp.int32, (rows, reach), 1).astype(F32) - HALO
        away = middle - own
        first = jnp.where(jnp.abs(away) <= HALO, 0.5 * jnp.exp(-away * away / spread_sq), 0.0)
        filt2[n] = jnp.dot(
            first, taps, precision=lax.Precision.HIGHEST, preferred_element_type=F32
        )
        band = lat + offset(n)
        inside = jnp.where((band >= 0) & (band < n_lat), 1.0, 0.0)
        target[pl.ds(n, 1), :] = meta[n, 2:3, :]
        scale[pl.ds(n, 1), :] = meta[n, 3:4, :]
        live[pl.ds(n, 1), :] = meta[n, 4:5, :] * inside

    image_acc[...] = jnp.zeros_like(image_acc)
    control_ref[...] = jnp.zeros_like(control_ref)

    def scattered(filter_ref, bands, first):
        acc[...] = jnp.zeros_like(acc)

        @pl.loop(0, bands)
        def _(n):
            @pl.when(first & (n > 0))
            def _():
                value_copy(n).wait_recv()

            @pl.when(first)
            def _():
                values = jnp.broadcast_to(bvals[n][:, None, :], (members, rows, slots))
                spread[n] = values.reshape(flat, slots).astype(BF16)

            factor = filter_ref[n] * q_now[pl.ds(n, 1), :]
            value = spread[n].astype(F32).reshape(members, rows, slots) * factor[None]
            high, low = halves(value.reshape(flat, slots))
            acc[...] += lax.dot_general(
                jnp.concatenate([high, low], axis=0),
                onehot[n],
                (((1,), (1,)), ((), ())),
                preferred_element_type=F32,
            )

        return acc[:flat] + acc[flat:]

    def filtered(value, which):
        high, low = halves(value)
        both = jnp.concatenate([high, low], axis=0)
        vext[:, PAD : PAD + cols] = both
        vext[:, :PAD] = both[:, cols - PAD :]
        vext[:, PAD + cols :] = both[:, :PAD]
        blocks = []
        for j in range(cols // BLOCK):
            window = vext[:, j * BLOCK : j * BLOCK + BLOCK + 2 * PAD]
            product = dot(window, win_ref[2 * which])
            blocks.append(
                product[:flat] + product[flat:] + dot(window[:flat], win_ref[2 * which + 1])
            )
        return blocks

    def send_image(k):
        @pl.loop(1, n_mem)
        def _(r):
            to = lax.rem(mem + r, n_mem)
            width = inc_ref.shape[1]
            part = pl.ds(pl.multiple_of(to * width, 128), width)
            remote(
                image.at[k, :, part], irecv.at[k, r - 1], i_send.at[k], i_recv.at[k], mem_peer(r)
            ).start()

    @pl.loop(0, ITERS)
    def _(t):
        last = t == ITERS - 1
        bounded = jnp.tanh((target[...] - observed[...]) / scale[...])
        q_now[...] = live[...] * (scale[...] * bounded) - summed[...]
        weight[...] = (live[...] * (1.0 - bounded * bounded))[0:1]

        for j, block in enumerate(filtered(scattered(filt2, NEAR, t == 0), 1)):
            high, low = halves(block)
            vwide[:, j * BLOCK : (j + 1) * BLOCK] = jnp.concatenate([high, low], axis=0)
        vwide[:, cols:] = vwide[:, :PAD]

        seen = dot(vwide[:, :cols], onehot[0])
        hits_part = c * jnp.sum(
            chosen[...].astype(F32) * (seen[:flat] + seen[flat:]), axis=0, keepdims=True
        )
        hsend[t] = hits_part

        @pl.loop(1, n_mem)
        def _(r):
            remote(
                hsend.at[t], hrecv.at[t, r - 1], h_send.at[t], h_recv.at[t], mem_peer(r)
            ).start()

        at_t = jnp.where(last, 1, 0)
        for j in range(fine_cols // 256):
            wide = dot(vwide[:, 128 * j : 128 * j + 256], widen_ref[...])
            wide = (wide[:flat] + wide[flat:]).reshape(members, rows, 256)
            here = slice(256 * j, 256 * (j + 1))
            for e in range(2):
                pert = picked[e * flat : (e + 1) * flat, here].astype(F32)
                total = c * jnp.sum(pert.reshape(members, rows, 256) * wide, axis=0)
                image[at_t, e * rows : (e + 1) * rows, here] = total

        @pl.when(last)
        def _():
            send_image(1)

        wait_all(hrecv.at[t], h_recv.at[t])
        hits = hits_part + jnp.sum(hrecv[t], axis=0)
        q_own = q_now[0:1, :]
        gg_part = q_own * hits
        cc_part = weight[...] * hits * hits
        width = 128
        ssend[t, :, :width] = sum(
            gg_part[:, i : i + width] for i in range(0, slots, width)
        )
        ssend[t, :, width:] = sum(
            cc_part[:, i : i + width] for i in range(0, slots, width)
        )

        @pl.loop(1, n_lat)
        def _(r):
            remote(
                ssend.at[t], srecv.at[t, r - 1], s_send.at[t], s_recv.at[t], lat_peer(r)
            ).start()

        hnear[t, 0] = hits

        def near_hits(n):
            return remote(
                hnear.at[t, 0],
                hnear.at[t, n],
                n_send.at[t, n - 1],
                n_recv.at[t, n - 1],
                near_peer(n),
            )

        @pl.loop(1, NEAR)
        def _(n):
            near_hits(n).start()

        for j, block in enumerate(filtered(scattered(filt, 3, t < 0), 0)):
            along[:, j * BLOCK : (j + 1) * BLOCK] = block

        wait_all(srecv.at[t], s_recv.at[t])
        sums = ssend[t] + jnp.sum(srecv[t], axis=0)
        gg = jnp.maximum(jnp.sum(sums[:, :width], axis=1, keepdims=True), 0.0)
        cc = jnp.sum(sums[:, width:], axis=1, keepdims=True)
        step = gg / (gg + cc + 1e-6)

        control_ref[...] += step[None] * along[...].reshape(members, rows, cols)
        summed[...] += step * q_now[...]
        observed[0:1, :] += step * hits

        @pl.loop(1, NEAR)
        def _(n):
            near_hits(n).wait_recv()
            observed[pl.ds(n, 1), :] += step * hnear[t, n]

        @pl.when(jnp.logical_not(last))
        def _():
            image_acc[...] += step * image[0]

        @pl.when(t == ITERS - 2)
        def _():
            image[0] = image_acc[...]
            send_image(0)

        @pl.when(last)
        def _():
            width = inc_ref.shape[1]
            part = pl.ds(pl.multiple_of(mem * width, 128), width)
            wait_all(irecv.at[0], i_recv.at[0])
            wait_all(irecv.at[1], i_recv.at[1])
            before = image[0, :, part] + jnp.sum(irecv[0], axis=0)
            now = image[1, :, part] + jnp.sum(irecv[1], axis=0)
            total = before + step * now
            for e in range(2):
                inc_ref[pl.ds(e, rows, 2), :] = total[e * rows : (e + 1) * rows]

    @pl.loop(1, NEAR)
    def _(n):
        meta_copy(n).wait_send()
        value_copy(n).wait_send()

    @pl.loop(0, ITERS)
    def _(t):
        wait_all(hrecv.at[t], h_send.at[t])
        wait_all(srecv.at[t], s_send.at[t])

        @pl.loop(1, NEAR)
        def _(n):
            wait_all(hnear.at[t, n], n_send.at[t, n - 1])

    wait_all(irecv.at[0], i_send.at[0])
    wait_all(irecv.at[1], i_send.at[1])


def on_device(n_mem, n_lat, windows, pert, cells, count, innov, scale):
    members, fine_rows, fine_cols = pert.shape
    rows, cols = fine_rows // 2, fine_cols // 2
    slots = cells.shape[1]
    flat = members * rows
    width = fine_cols // n_mem
    vmem = pl.BlockSpec(memory_space=pltpu.VMEM)
    scratch = [
        pltpu.VMEM((NEAR, 8, slots), F32),
        pltpu.VMEM((NEAR, members, slots), F32),
        pltpu.VMEM((NEAR, flat, slots), BF16),
        pltpu.VMEM((flat, slots), BF16),
        pltpu.VMEM((2 * flat, fine_cols), BF16),
        pltpu.VMEM((NEAR, cols, slots), BF16),
        pltpu.VMEM((NEAR, rows, slots), F32),
        pltpu.VMEM((NEAR, rows, slots), F32),
        pltpu.VMEM((8, slots), F32),
        pltpu.VMEM((8, slots), F32),
        pltpu.VMEM((8, slots), F32),
        pltpu.VMEM((8, slots), F32),
        pltpu.VMEM((8, slots), F32),
        pltpu.VMEM((8, slots), F32),
        pltpu.VMEM((1, slots), F32),
        pltpu.VMEM((2 * flat, cols), F32),
        pltpu.VMEM((2 * flat, cols + 2 * PAD), BF16),
        pltpu.VMEM((2 * flat, cols + PAD), BF16),
        pltpu.VMEM((flat, cols), F32),
        pltpu.VMEM((2, fine_rows, fine_cols), F32),
        pltpu.VMEM((fine_rows, fine_cols), F32),
        pltpu.VMEM((ITERS, 1, slots), F32),
        pltpu.VMEM((ITERS, n_mem - 1, 1, slots), F32),
        pltpu.VMEM((ITERS, NEAR, 1, slots), F32),
        pltpu.VMEM((ITERS, 1, 256), F32),
        pltpu.VMEM((ITERS, n_lat - 1, 1, 256), F32),
        pltpu.VMEM((2, n_mem - 1, fine_rows, width), F32),
    ]
    scratch += [pltpu.SemaphoreType.DMA((NEAR - 1,))] * 4
    scratch += [pltpu.SemaphoreType.DMA((ITERS,))] * 2
    scratch += [pltpu.SemaphoreType.DMA((ITERS, NEAR - 1))] * 2
    scratch += [pltpu.SemaphoreType.DMA((ITERS,))] * 2
    scratch += [pltpu.SemaphoreType.DMA((2,))] * 2
    control, increment = pl.pallas_call(
        functools.partial(body, n_mem, n_lat),
        out_shape=(
            jax.ShapeDtypeStruct((members, rows, cols), F32),
            jax.ShapeDtypeStruct((fine_rows, width), F32),
        ),
        in_specs=[vmem, pl.BlockSpec(memory_space=pltpu.SMEM)] + [vmem] * 6,
        out_specs=(vmem, vmem),
        scratch_shapes=scratch,
        compiler_params=pltpu.CompilerParams(
            collective_id=0, has_side_effects=True, vmem_limit_bytes=60 * 2**20
        ),
    )(
        cells,
        count,
        innov,
        scale,
        pert,
        jnp.asarray(split_rows_matrix(members, fine_rows)),
        jnp.asarray(windows),
        jnp.asarray(widen_matrix()),
    )
    return control, increment


def solution(mesh):
    n_mem, n_lat = mesh.shape["mem"], mesh.shape["lat"]

    def run(pert, cells, count, innov, scale):
        windows = window_matrices(pert.shape[2] // 2)
        return on_device(n_mem, n_lat, windows, pert, cells, count, innov, scale)

    return jax.shard_map(
        run,
        mesh=mesh,
        in_specs=(P("mem", "lat", None), P("lat", None), P("lat"), P("lat", None), P("lat", None)),
        out_specs=(P("mem", "lat", None), P("lat", "mem")),
        check_vma=False,
    )
```

time: 609 us -> 103 us (0.17); the launches traced: 599 us -> 102 us
  blocking collectives: 186 us -> 0 us
  local copies, waits for them, and re-layouts: 170 us -> 2.49 us
  Pallas kernels: 0 us -> 98.6 us
  other arithmetic: 75.7 us -> 0 us
  waiting for transfers between devices: 65.8 us -> 0 us
  starting transfers between devices: 60.7 us -> 0 us
  matrix products: 32.5 us -> 0 us
  between operations: 8.29 us -> 1.29 us
    psum x15 -> x0, blocking collectives: 166 us -> none  [one_axis_at_a_time(): return functools.reduce(lax.psum, axes, value)]
    pallas_call x0 -> x1, Pallas kernels: none -> 98.6 us  [on_device(): pl.pallas_call(functools.partial(body, n_mem, n_lat), out_shape=(jax.Shap...]
    gather x3 -> x0, local copies, waits for them, and re-layouts: 50 us -> none  [on_device(): hits = over_copies(partial_image[row_index, col_index], MEM)]
    ppermute x12 -> x0, waiting for transfers between devices: 48.3 us -> none  [the longest x6 25.9 us: padded_2(): lax.ppermute(lax.slice_in_dim(block, block.shape[dim] - width, None, axis...]
    reshape x9 -> x0, local copies, waits for them, and re-layouts: 36.3 us -> none  [the longest x3 16.1 us: widen_lon(): jnp.stack([coarse, odd_part], axis=-1)]
    all_to_all x3 -> x0, starting transfers between devices: 34.3 us -> none  [the longest x2 22.5 us: sent_to_all(): lax.all_to_all(jnp.broadcast_to(value[None], (devices, *value.shape)), ax...]
    scatter-add x3 -> x0, other arithmetic: 34 us -> none  [on_device(): obs_field = jnp.zeros((fine_rows * lon_cells,), jnp.float32).at[obs_index...]
    dot_general x12 -> x0, matrix products: 32.5 us -> none  [the longest x3 13.1 us: on_device(): jnp.dot(folded, circulant, precision=lax.Precision.HIGHEST, preferred_ele...]
  transfers between devices with their start and end apart: 15 -> 0, of which waited for: 13 -> 0; matrix products, arithmetic and copies ran while one was open for 2% -> 0% of each run, Pallas kernels for 0% -> 0%
where the time goes in v1:
time: 103 us; the launch traced here: 102 us
  Pallas kernels  98.6 us (96%)
  local copies, waits for them, and re-layouts  2.49 us (2%)
  between operations  1.29 us (1%)
    pallas_call x1, Pallas kernels, on_device(): pl.pallas_call(functools.partial(body, n_mem, n_lat), out_shape=(jax.Shap...  98.6 us
    unnamed x4, local copies, waits for them, and re-layouts  2.49 us

profile of v1, /device:TPU:1, one launch (start us, length us, event | category | flops | bytes accessed | tf_op | source)
XLA Modules:
  0.0 102.4 jit_solution(1751474903412156738)
XLA Ops:
  1.3 98.6 %shard_map.95 = (f32[16,8,1024]{2,1,0:T(8,128)}, f32[16,128]{1,0:T(8,128)}) custom-call(s32[1,2048]{1,0:T(1,128)} %cells_ref.1, s32[1]{0:T(128)S(6)} %copy.12.count_ref, f32[1,2048]{1,0:T(1,128)} %innov_ref.1, f32[1,2048]{1,0:T(1,128)} %scale_ref.1, bf16[16,16,2048]{2,1,0:T(8,128)(2,1)} %pert_ref.1, bf16[256,256]{1,0:T(8,128)(2,1)} %constant.6.clone.sel_ref, ...), custom_call_target="tpu_custom_call" | custom-call | tf_op jit(solution)/shard_map/pallas_call | solution.py:490
  99.9 0.0 copy-start
  99.9 1.9 %copy.13 = f32[16,8,1024]{2,1,0:T(8,128)} copy(f32[16,8,1024]{2,1,0:T(8,128)} %get-tuple-element.4) | data formatting | bytes 1048576
  101.8 0.0 copy-done
  101.8 0.6 copy.14
Async XLA Ops:
  99.9 1.9 %copy-start = (f32[16,128]{1,0:T(8,128)S(1)}, f32[16,128]{1,0:T(8,128)}, u32[]{:S(2)}) copy-start(f32[16,128]{1,0:T(8,128)} %get-tuple-element.5) | copy-start | bytes 24580

commit v2 on v1

--- a/solution.py
+++ b/solution.py
@@ -155,19 +155,16 @@
         pl.semaphore_signal(barrier, inc=1, device_id=lat_peer(r), device_id_type=MESH)
 
     cells = cells_ref[...]
-    row = cells >> (fine_cols.bit_length() - 1)
-    col = cells & (fine_cols - 1)
-    coarse_row = (row >> 1).astype(F32)
     slot_id = lax.broadcasted_iota(jnp.int32, (1, slots), 1)
-    meta[0, 0:1, :] = col.astype(F32) * 0.5
-    meta[0, 1:2, :] = coarse_row
-    meta[0, 2:3, :] = innov_ref[...]
-    meta[0, 3:4, :] = scale_ref[...]
-    meta[0, 4:5, :] = jnp.where(slot_id < count_ref[0], 1.0, 0.0)
-    meta[0, 5:6, :] = col.astype(F32)
-    meta[0, 6:7, :] = (row & 1).astype(F32)
-    meta[0, 7:8, :] = jnp.zeros((1, slots), F32)
-    pl.semaphore_wait(barrier, n_mem + n_lat - 2)
+    meta[0, 0:1, :] = cells.astype(F32)
+    meta[0, 1:2, :] = innov_ref[...]
+    meta[0, 2:3, :] = scale_ref[...]
+    meta[0, 3:4, :] = jnp.where(slot_id < count_ref[0], 1.0, 0.0)
+
+    def place_of(n, at):
+        cell = meta[n, 0:1, at]
+        fine_row = jnp.floor(cell * (1.0 / fine_cols))
+        return fine_row, cell - fine_row * float(fine_cols)
 
     def near_peer(n):
         return {"lat": lax.rem(lat - offset(n) + n_lat, n_lat)}
@@ -181,10 +178,6 @@
         return remote(
             bvals.at[0], bvals.at[n], b_send.at[n - 1], b_recv.at[n - 1], near_peer(n)
         )
-
-    @pl.loop(1, NEAR)
-    def _(n):
-        meta_copy(n).start()
 
     @pl.loop(0, fine_cols // BLOCK)
     def _(j):
@@ -196,19 +189,17 @@
     @pl.loop(0, slots // BLOCK)
     def _(j):
         at = pl.ds(pl.multiple_of(j * BLOCK, BLOCK), BLOCK)
-        column = meta[0, 5:6, at]
+        fine_row, column = place_of(0, at)
+        coarse_row = jnp.floor(fine_row * 0.5)
         place = lax.broadcasted_iota(jnp.int32, (fine_cols, BLOCK), 0).astype(F32)
         hit = jnp.where(place == column, 1.0, 0.0).astype(BF16)
         both = dot(picked[...], hit)
-        value = jnp.where(meta[0, 6:7, at] > 0.5, both[flat:], both[:flat])
-        own = lax.broadcasted_iota(jnp.int32, (rows, BLOCK), 0).astype(F32) == meta[0, 1:2, at]
+        odd = fine_row - 2.0 * coarse_row
+        value = jnp.where(odd > 0.5, both[flat:], both[:flat])
+        own = lax.broadcasted_iota(jnp.int32, (rows, BLOCK), 0).astype(F32) == coarse_row
         value = jnp.where(own[None], value.reshape(members, rows, BLOCK), 0.0)
         chosen[:, at] = value.reshape(flat, BLOCK).astype(BF16)
         bvals[0, :, at] = jnp.sum(value, axis=1)
-
-    @pl.loop(1, NEAR)
-    def _(n):
-        value_copy(n).start()
 
     target[...] = jnp.zeros_like(target)
     scale[...] = jnp.ones_like(scale)
@@ -216,21 +207,18 @@
     observed[...] = jnp.zeros_like(observed)
     summed[...] = jnp.zeros_like(summed)
 
-    @pl.loop(0, NEAR)
-    def _(n):
-        @pl.when(n > 0)
-        def _():
-            meta_copy(n).wait_recv()
-
-        x = meta[n, 0:1, :]
+    def prepare(n):
+        fine_row, column = place_of(n, slice(None))
+        x = column * 0.5
         step = 128
+        place16 = lax.broadcasted_iota(jnp.int32, (step, slots), 0).astype(F32).astype(BF16)
 
         @pl.loop(0, cols // step)
         def _(j):
             start = pl.multiple_of(j * step, step)
-            place = (lax.broadcasted_iota(jnp.int32, (step, slots), 0) + start).astype(F32)
-            hat = jnp.maximum(1.0 - jnp.abs(x - place), 0.0)
-            onehot[n, pl.ds(start, step), :] = hat.astype(BF16)
+            near = jnp.clip(x - start.astype(F32), -2.0, step + 1.0).astype(BF16)
+            apart = jnp.abs(near - place16)
+            onehot[n, pl.ds(start, step), :] = jnp.maximum(BF16(1.0) - apart, BF16(0.0))
 
         place = lax.broadcasted_iota(jnp.int32, (16, slots), 0).astype(F32)
         hat = jnp.maximum(
@@ -241,8 +229,8 @@
         reach = rows + 2 * HALO
         between = lax.broadcasted_iota(jnp.int32, (reach, slots), 0) - HALO
         whole = between + lat * rows
-        there = meta[n, 1:2, :] + (offset(n) * rows).astype(F32)
-        apart = between.astype(F32) - there
+        shift = jnp.asarray(offset(n) * rows, jnp.int32).astype(F32)
+        apart = between.astype(F32) - (jnp.floor(fine_row * 0.5) + shift)
         spread_sq = 2.0 * (HALO / 2.0) ** 2
         taps = jnp.where(
             (jnp.abs(apart) <= HALO) & (whole >= 0) & (whole < n_lat * rows),
@@ -259,9 +247,32 @@
         )
         band = lat + offset(n)
         inside = jnp.where((band >= 0) & (band < n_lat), 1.0, 0.0)
-        target[pl.ds(n, 1), :] = meta[n, 2:3, :]
-        scale[pl.ds(n, 1), :] = meta[n, 3:4, :]
-        live[pl.ds(n, 1), :] = meta[n, 4:5, :] * inside
+        target[pl.ds(n, 1), :] = meta[n, 1:2, :]
+        scale[pl.ds(n, 1), :] = meta[n, 2:3, :]
+        live[pl.ds(n, 1), :] = meta[n, 3:4, :] * inside
+
+    pl.semaphore_wait(barrier, n_mem + n_lat - 2)
+
+    @pl.loop(1, NEAR)
+    def _(n):
+        meta_copy(n).start()
+
+    @pl.loop(1, 3)
+    def _(n):
+        value_copy(n).start()
+
+    @pl.loop(0, NEAR)
+    def _(n):
+        @pl.when(n > 0)
+        def _():
+            meta_copy(n).wait_recv()
+
+        @pl.when(n == 1)
+        def _():
+            value_copy(3).start()
+            value_copy(4).start()
+
+        prepare(n)
 
     image_acc[...] = jnp.zeros_like(image_acc)
     control_ref[...] = jnp.zeros_like(control_ref)
@@ -374,7 +385,9 @@
                 ssend.at[t], srecv.at[t, r - 1], s_send.at[t], s_recv.at[t], lat_peer(r)
             ).start()
 
-        hnear[t, 0] = hits
+        @pl.when(jnp.logical_not(last))
+        def _():
+            hnear[t, 0] = hits
 
         def near_hits(n):
             return remote(
@@ -385,9 +398,11 @@
                 near_peer(n),
             )
 
-        @pl.loop(1, NEAR)
-        def _(n):
-            near_hits(n).start()
+        @pl.when(jnp.logical_not(last))
+        def _():
+            @pl.loop(1, NEAR)
+            def _(n):
+                near_hits(n).start()
 
         for j, block in enumerate(filtered(scattered(filt, 3, t < 0), 0)):
             along[:, j * BLOCK : (j + 1) * BLOCK] = block
@@ -402,13 +417,13 @@
         summed[...] += step * q_now[...]
         observed[0:1, :] += step * hits
 
-        @pl.loop(1, NEAR)
-        def _(n):
-            near_hits(n).wait_recv()
-            observed[pl.ds(n, 1), :] += step * hnear[t, n]
-
         @pl.when(jnp.logical_not(last))
         def _():
+            @pl.loop(1, NEAR)
+            def _(n):
+                near_hits(n).wait_recv()
+                observed[pl.ds(n, 1), :] += step * hnear[t, n]
+
             image_acc[...] += step * image[0]
 
         @pl.when(t == ITERS - 2)
@@ -438,9 +453,11 @@
         wait_all(hrecv.at[t], h_send.at[t])
         wait_all(srecv.at[t], s_send.at[t])
 
-        @pl.loop(1, NEAR)
-        def _(n):
-            wait_all(hnear.at[t, n], n_send.at[t, n - 1])
+        @pl.when(t < ITERS - 1)
+        def _():
+            @pl.loop(1, NEAR)
+            def _(n):
+                wait_all(hnear.at[t, n], n_send.at[t, n - 1])
 
     wait_all(irecv.at[0], i_send.at[0])
     wait_all(irecv.at[1], i_send.at[1])
@@ -454,7 +471,7 @@
     width = fine_cols // n_mem
     vmem = pl.BlockSpec(memory_space=pltpu.VMEM)
     scratch = [
-        pltpu.VMEM((NEAR, 8, slots), F32),
+        pltpu.VMEM((NEAR, 4, slots), F32),
         pltpu.VMEM((NEAR, members, slots), F32),
         pltpu.VMEM((NEAR, flat, slots), BF16),
         pltpu.VMEM((flat, slots), BF16),
@@ -477,14 +494,14 @@
         pltpu.VMEM((fine_rows, fine_cols), F32),
         pltpu.VMEM((ITERS, 1, slots), F32),
         pltpu.VMEM((ITERS, n_mem - 1, 1, slots), F32),
-        pltpu.VMEM((ITERS, NEAR, 1, slots), F32),
+        pltpu.VMEM((ITERS - 1, NEAR, 1, slots), F32),
         pltpu.VMEM((ITERS, 1, 256), F32),
         pltpu.VMEM((ITERS, n_lat - 1, 1, 256), F32),
         pltpu.VMEM((2, n_mem - 1, fine_rows, width), F32),
     ]
     scratch += [pltpu.SemaphoreType.DMA((NEAR - 1,))] * 4
     scratch += [pltpu.SemaphoreType.DMA((ITERS,))] * 2
-    scratch += [pltpu.SemaphoreType.DMA((ITERS, NEAR - 1))] * 2
+    scratch += [pltpu.SemaphoreType.DMA((ITERS - 1, NEAR - 1))] * 2
     scratch += [pltpu.SemaphoreType.DMA((ITERS,))] * 2
     scratch += [pltpu.SemaphoreType.DMA((2,))] * 2
     control, increment = pl.pallas_call(

time: 103 us -> 97.8 us (0.950)
  Pallas kernels: 98.6 us -> 93.8 us
    pallas_call x1, Pallas kernels: 98.6 us -> 93.8 us  [on_device(): pl.pallas_call(functools.partial(body, n_mem, n_lat), out_shape=(jax.Shap...]
where the time goes in v2:
time: 97.8 us; the launch traced here: 97.6 us
  Pallas kernels  93.8 us (96%)
  local copies, waits for them, and re-layouts  2.49 us (3%)
  between operations  1.29 us (1%)
    pallas_call x1, Pallas kernels, on_device(): pl.pallas_call(functools.partial(body, n_mem, n_lat), out_shape=(jax.Shap...  93.8 us
    unnamed x4, local copies, waits for them, and re-layouts  2.49 us

profile of v2, /device:TPU:1, one launch (start us, length us, event | category | flops | bytes accessed | tf_op | source)
XLA Modules:
  0.0 97.6 jit_solution(16736172249387496015)
XLA Ops:
  1.3 93.8 %shard_map.95 = (f32[16,8,1024]{2,1,0:T(8,128)}, f32[16,128]{1,0:T(8,128)}) custom-call(s32[1,2048]{1,0:T(1,128)} %cells_ref.1, s32[1]{0:T(128)S(6)} %copy.12.count_ref, f32[1,2048]{1,0:T(1,128)} %innov_ref.1, f32[1,2048]{1,0:T(1,128)} %scale_ref.1, bf16[16,16,2048]{2,1,0:T(8,128)(2,1)} %pert_ref.1, bf16[256,256]{1,0:T(8,128)(2,1)} %constant.6.clone.sel_ref, ...), custom_call_target="tpu_custom_call" | custom-call | tf_op jit(solution)/shard_map/pallas_call | solution.py:507
  95.1 0.0 copy-start
  95.1 1.9 %copy.13 = f32[16,8,1024]{2,1,0:T(8,128)} copy(f32[16,8,1024]{2,1,0:T(8,128)} %get-tuple-element.4) | data formatting | bytes 1048576
  97.0 0.0 copy-done
  97.0 0.6 copy.14
Async XLA Ops:
  95.1 1.9 %copy-start = (f32[16,128]{1,0:T(8,128)S(1)}, f32[16,128]{1,0:T(8,128)}, u32[]{:S(2)}) copy-start(f32[16,128]{1,0:T(8,128)} %get-tuple-element.5) | copy-start | bytes 24580

commit v3 on v2

--- a/solution.py
+++ b/solution.py
@@ -14,6 +14,7 @@
 ITERS = 3
 NEAR = 5
 BLOCK = 256
+STRIDE = 255
 PAD = 128
 F32 = jnp.float32
 BF16 = jnp.bfloat16
@@ -81,6 +82,16 @@
     chosen,
     picked,
     onehot,
+    tile,
+    columns,
+    last_chunk,
+    keys,
+    rank,
+    unsorted,
+    left_even,
+    left_odd,
+    running,
+    whole,
     filt,
     filt2,
     target,
@@ -156,10 +167,49 @@
 
     cells = cells_ref[...]
     slot_id = lax.broadcasted_iota(jnp.int32, (1, slots), 1)
-    meta[0, 0:1, :] = cells.astype(F32)
-    meta[0, 1:2, :] = innov_ref[...]
-    meta[0, 2:3, :] = scale_ref[...]
-    meta[0, 3:4, :] = jnp.where(slot_id < count_ref[0], 1.0, 0.0)
+    chunks = slots // BLOCK
+    blocks = -(-cols // STRIDE)
+    tiles = chunks + blocks - 1
+
+    column_id = cells & (fine_cols - 1)
+    key = (column_id * slots + slot_id).astype(F32)
+    keys[...] = jnp.broadcast_to(key, (128, slots)).T
+    rank[...] = key
+
+    @pl.loop(0, slots // 128)
+    def _(j):
+        at = pl.ds(pl.multiple_of(j * 128, 128), 128)
+        below = jnp.where(keys[...] < rank[:, at], 1.0, 0.0)
+        rank[:, at] = jnp.sum(below, axis=0, keepdims=True)
+
+    def thirds(value):
+        high = value.astype(BF16).astype(F32)
+        middle = (value - high).astype(BF16).astype(F32)
+        return [high, middle, value - high - middle]
+
+    given = jnp.concatenate(
+        [(cells >> 8).astype(F32), (cells & 255).astype(F32)]
+        + thirds(innov_ref[...])
+        + thirds(scale_ref[...])
+        + [jnp.where(slot_id < count_ref[0], 1.0, 0.0)]
+        + [jnp.zeros((7, slots), F32)],
+        axis=0,
+    )
+    unsorted[...] = given.astype(BF16)
+
+    @pl.loop(0, chunks)
+    def _(j):
+        start = pl.multiple_of(j * BLOCK, BLOCK)
+        to = (lax.broadcasted_iota(jnp.int32, (BLOCK, slots), 0) + start).astype(F32)
+        move = jnp.where(to == rank[...], 1.0, 0.0).astype(BF16)
+        moved = lax.dot_general(
+            unsorted[...], move, (((1,), (1,)), ((), ())), preferred_element_type=F32
+        )
+        at = pl.ds(start, BLOCK)
+        meta[0, 0:1, at] = moved[0:1] * 256.0 + moved[1:2]
+        meta[0, 1:2, at] = moved[2:3] + moved[3:4] + moved[4:5]
+        meta[0, 2:3, at] = moved[5:6] + moved[6:7] + moved[7:8]
+        meta[0, 3:4, at] = moved[8:9]
 
     def place_of(n, at):
         cell = meta[n, 0:1, at]
@@ -207,9 +257,14 @@
     observed[...] = jnp.zeros_like(observed)
     summed[...] = jnp.zeros_like(summed)
 
-    def prepare(n):
-        fine_row, column = place_of(n, slice(None))
-        x = column * 0.5
+    def block_of(n, p):
+        block = jnp.int32(0)
+        for j in range(blocks - 1):
+            block += jnp.where(last_chunk[n, j] + j < p, 1, 0).astype(jnp.int32)
+        return jnp.maximum(block, p - (chunks - 1))
+
+    def prepare_own():
+        x = place_of(0, slice(None))[1] * 0.5
         step = 128
         place16 = lax.broadcasted_iota(jnp.int32, (step, slots), 0).astype(F32).astype(BF16)
 
@@ -218,22 +273,37 @@
             start = pl.multiple_of(j * step, step)
             near = jnp.clip(x - start.astype(F32), -2.0, step + 1.0).astype(BF16)
             apart = jnp.abs(near - place16)
-            onehot[n, pl.ds(start, step), :] = jnp.maximum(BF16(1.0) - apart, BF16(0.0))
+            onehot[pl.ds(start, step), :] = jnp.maximum(BF16(1.0) - apart, BF16(0.0))
 
         place = lax.broadcasted_iota(jnp.int32, (16, slots), 0).astype(F32)
         hat = jnp.maximum(
             jnp.maximum(1.0 - jnp.abs(x - place), 1.0 - jnp.abs(x - (place + float(cols)))), 0.0
         )
-        onehot[n, 0:16, :] = hat.astype(BF16)
+        onehot[0:16, :] = hat.astype(BF16)
+
+    def prepare(n):
+        fine_row, column = place_of(n, slice(None))
+        x = column * 0.5
+        for j in range(chunks):
+            columns[j] = x[:, j * BLOCK : (j + 1) * BLOCK]
+        for j in range(blocks - 1):
+            count = jnp.sum(jnp.where(x < float(STRIDE * (j + 1)), 1.0, 0.0)).astype(jnp.int32)
+            last_chunk[n, j] = jnp.clip(((count + BLOCK - 1) >> 8) - 1, 0, chunks - 1)
+        for p in range(tiles):
+            block = block_of(n, p)
+            local = columns[p - block] - (block * STRIDE).astype(F32)
+            local = jnp.where((local >= 0.0) & (local < float(STRIDE)), local, -9.0)
+            place = lax.broadcasted_iota(jnp.int32, (BLOCK, BLOCK), 0).astype(F32)
+            tile[n, p] = jnp.maximum(1.0 - jnp.abs(local - place), 0.0).astype(BF16)
 
         reach = rows + 2 * HALO
         between = lax.broadcasted_iota(jnp.int32, (reach, slots), 0) - HALO
-        whole = between + lat * rows
+        global_row = between + lat * rows
         shift = jnp.asarray(offset(n) * rows, jnp.int32).astype(F32)
         apart = between.astype(F32) - (jnp.floor(fine_row * 0.5) + shift)
         spread_sq = 2.0 * (HALO / 2.0) ** 2
         taps = jnp.where(
-            (jnp.abs(apart) <= HALO) & (whole >= 0) & (whole < n_lat * rows),
+            (jnp.abs(apart) <= HALO) & (global_row >= 0) & (global_row < n_lat * rows),
             (0.5 * c) * jnp.exp(-apart * apart / spread_sq),
             0.0,
         )
@@ -251,6 +321,7 @@
         scale[pl.ds(n, 1), :] = meta[n, 2:3, :]
         live[pl.ds(n, 1), :] = meta[n, 3:4, :] * inside
 
+    prepare_own()
     pl.semaphore_wait(barrier, n_mem + n_lat - 2)
 
     @pl.loop(1, NEAR)
@@ -277,31 +348,65 @@
     image_acc[...] = jnp.zeros_like(image_acc)
     control_ref[...] = jnp.zeros_like(control_ref)
 
+    lefts = (left_even, left_odd)
+
     def scattered(filter_ref, bands, first):
         acc[...] = jnp.zeros_like(acc)
 
-        @pl.loop(0, bands)
-        def _(n):
-            @pl.when(first & (n > 0))
-            def _():
-                value_copy(n).wait_recv()
-
+        def values_of(n):
             @pl.when(first)
             def _():
+                if n > 0:
+                    value_copy(n).wait_recv()
                 values = jnp.broadcast_to(bvals[n][:, None, :], (members, rows, slots))
                 spread[n] = values.reshape(flat, slots).astype(BF16)
 
-            factor = filter_ref[n] * q_now[pl.ds(n, 1), :]
-            value = spread[n].astype(F32).reshape(members, rows, slots) * factor[None]
-            high, low = halves(value.reshape(flat, slots))
-            acc[...] += lax.dot_general(
-                jnp.concatenate([high, low], axis=0),
-                onehot[n],
-                (((1,), (1,)), ((), ())),
-                preferred_element_type=F32,
-            )
-
-        return acc[:flat] + acc[flat:]
+        def weigh(n):
+            left = lefts[n % 2]
+            factor = filter_ref[n] * q_now[n : n + 1, :]
+            for j in range(chunks):
+                here = slice(j * BLOCK, (j + 1) * BLOCK)
+                value = spread[n, :, here].astype(F32).reshape(members, rows, BLOCK)
+                high, low = halves((value * factor[None, :, here]).reshape(flat, BLOCK))
+                left[j, :flat] = high
+                left[j, flat:] = low
+
+        def multiply(n):
+            left = lefts[n % 2]
+            before = None
+            for p in range(tiles):
+                block = block_of(n, p)
+                product = lax.dot_general(
+                    left[p - block],
+                    tile[n, p],
+                    (((1,), (1,)), ((), ())),
+                    preferred_element_type=F32,
+                )
+                total = product[:flat] + product[flat:]
+                if p > 0:
+                    total += jnp.where(block == before, 1.0, 0.0) * running[p - 1]
+                running[p] = total
+                before = block
+            for j in range(blocks):
+                end = last_chunk[n, j] + j if j < blocks - 1 else tiles - 1
+                acc[j] += running[end]
+
+        values_of(0)
+        weigh(0)
+        for n in range(bands):
+            if n + 1 < bands:
+                values_of(n + 1)
+                weigh(n + 1)
+            multiply(n)
+
+        whole[...] = jnp.zeros_like(whole)
+        whole[:, :BLOCK] = acc[0]
+        for j in range(1, blocks):
+            wide = jnp.concatenate([acc[j], jnp.zeros((flat, 128), F32)], axis=1)
+            start = BLOCK * j - 128
+            whole[:, start : start + BLOCK + 128] += pltpu.roll(wide, 128 - j, 1)
+        whole[:, :128] += whole[:, cols : cols + 128]
+        return whole[:, :cols]
 
     def filtered(value, which):
         high, low = halves(value)
@@ -340,7 +445,7 @@
             vwide[:, j * BLOCK : (j + 1) * BLOCK] = jnp.concatenate([high, low], axis=0)
         vwide[:, cols:] = vwide[:, :PAD]
 
-        seen = dot(vwide[:, :cols], onehot[0])
+        seen = dot(vwide[:, :cols], onehot[...])
         hits_part = c * jnp.sum(
             chosen[...].astype(F32) * (seen[:flat] + seen[flat:]), axis=0, keepdims=True
         )
@@ -469,6 +574,9 @@
     slots = cells.shape[1]
     flat = members * rows
     width = fine_cols // n_mem
+    chunks = slots // BLOCK
+    blocks = -(-cols // STRIDE)
+    tiles = chunks + blocks - 1
     vmem = pl.BlockSpec(memory_space=pltpu.VMEM)
     scratch = [
         pltpu.VMEM((NEAR, 4, slots), F32),
@@ -476,7 +584,17 @@
         pltpu.VMEM((NEAR, flat, slots), BF16),
         pltpu.VMEM((flat, slots), BF16),
         pltpu.VMEM((2 * flat, fine_cols), BF16),
-        pltpu.VMEM((NEAR, cols, slots), BF16),
+        pltpu.VMEM((cols, slots), BF16),
+        pltpu.VMEM((NEAR, tiles, BLOCK, BLOCK), BF16),
+        pltpu.VMEM((chunks, 1, BLOCK), F32),
+        pltpu.SMEM((NEAR, 8), jnp.int32),
+        pltpu.VMEM((slots, 128), F32),
+        pltpu.VMEM((1, slots), F32),
+        pltpu.VMEM((16, slots), BF16),
+        pltpu.VMEM((chunks, 2 * flat, BLOCK), BF16),
+        pltpu.VMEM((chunks, 2 * flat, BLOCK), BF16),
+        pltpu.VMEM((tiles, flat, BLOCK), F32),
+        pltpu.VMEM((flat, cols + 256), F32),
         pltpu.VMEM((NEAR, rows, slots), F32),
         pltpu.VMEM((NEAR, rows, slots), F32),
         pltpu.VMEM((8, slots), F32),
@@ -486,7 +604,7 @@
         pltpu.VMEM((8, slots), F32),
         pltpu.VMEM((8, slots), F32),
         pltpu.VMEM((1, slots), F32),
-        pltpu.VMEM((2 * flat, cols), F32),
+        pltpu.VMEM((blocks, flat, BLOCK), F32),
         pltpu.VMEM((2 * flat, cols + 2 * PAD), BF16),
         pltpu.VMEM((2 * flat, cols + PAD), BF16),
         pltpu.VMEM((flat, cols), F32),

time: 97.8 us -> 101 us (1.033)
  Pallas kernels: 93.8 us -> 97.2 us
    pallas_call x1, Pallas kernels: 93.8 us -> 97.2 us  [on_device(): pl.pallas_call(functools.partial(body, n_mem, n_lat), out_shape=(jax.Shap...]
where the time goes in v3:
time: 101 us
  Pallas kernels  97.2 us (96%)
  local copies, waits for them, and re-layouts  2.49 us (2%)
  between operations  1.29 us (1%)
    pallas_call x1, Pallas kernels, on_device(): pl.pallas_call(functools.partial(body, n_mem, n_lat), out_shape=(jax.Shap...  97.2 us
    unnamed x4, local copies, waits for them, and re-layouts  2.49 us

profile of v3, /device:TPU:1, one launch (start us, length us, event | category | flops | bytes accessed | tf_op | source)
XLA Modules:
  0.0 101.0 jit_solution(16402689353144080137)
XLA Ops:
  1.3 97.2 %shard_map.95 = (f32[16,8,1024]{2,1,0:T(8,128)}, f32[16,128]{1,0:T(8,128)}) custom-call(s32[1,2048]{1,0:T(1,128)} %cells_ref.1, s32[1]{0:T(128)S(6)} %copy.12.count_ref, f32[1,2048]{1,0:T(1,128)} %innov_ref.1, f32[1,2048]{1,0:T(1,128)} %scale_ref.1, bf16[16,16,2048]{2,1,0:T(8,128)(2,1)} %pert_ref.1, bf16[256,256]{1,0:T(8,128)(2,1)} %constant.6.clone.sel_ref, ...), custom_call_target="tpu_custom_call" | custom-call | tf_op jit(solution)/shard_map/pallas_call | solution.py:625
  98.5 0.0 copy-start
  98.5 1.9 %copy.13 = f32[16,8,1024]{2,1,0:T(8,128)} copy(f32[16,8,1024]{2,1,0:T(8,128)} %get-tuple-element.4) | data formatting | bytes 1048576
  100.4 0.0 copy-done
  100.4 0.6 copy.14
Async XLA Ops:
  98.5 1.9 %copy-start = (f32[16,128]{1,0:T(8,128)S(1)}, f32[16,128]{1,0:T(8,128)}, u32[]{:S(2)}) copy-start(f32[16,128]{1,0:T(8,128)} %get-tuple-element.5) | copy-start | bytes 24580

commit v4 on v2

--- a/solution.py
+++ b/solution.py
@@ -17,6 +17,8 @@
 PAD = 128
 F32 = jnp.float32
 BF16 = jnp.bfloat16
+F8 = jnp.float8_e4m3fn
+ROOM = 32.0
 MESH = pl.DeviceIdType.MESH
 
 
@@ -56,6 +58,15 @@
 def halves(value):
     high = value.astype(BF16)
     return high, (value - high.astype(F32)).astype(BF16)
+
+
+def thirds(value):
+    parts = []
+    for _ in range(3):
+        part = value.astype(F8)
+        parts.append(part)
+        value = (value - part.astype(F32)) * 16.0
+    return jnp.concatenate(parts, axis=0)
 
 
 def dot(a, b):
@@ -81,6 +92,7 @@
     chosen,
     picked,
     onehot,
+    onehot8,
     filt,
     filt2,
     target,
@@ -217,14 +229,22 @@
         def _(j):
             start = pl.multiple_of(j * step, step)
             near = jnp.clip(x - start.astype(F32), -2.0, step + 1.0).astype(BF16)
-            apart = jnp.abs(near - place16)
-            onehot[n, pl.ds(start, step), :] = jnp.maximum(BF16(1.0) - apart, BF16(0.0))
-
-        place = lax.broadcasted_iota(jnp.int32, (16, slots), 0).astype(F32)
+            hat = jnp.maximum(BF16(1.0) - jnp.abs(near - place16), BF16(0.0))
+            onehot8[n, pl.ds(start, step), :] = hat.astype(F8)
+
+            @pl.when(n == 0)
+            def _():
+                onehot[pl.ds(start, step), :] = hat
+
+        place = lax.broadcasted_iota(jnp.int32, (32, slots), 0).astype(F32)
         hat = jnp.maximum(
             jnp.maximum(1.0 - jnp.abs(x - place), 1.0 - jnp.abs(x - (place + float(cols)))), 0.0
         )
-        onehot[n, 0:16, :] = hat.astype(BF16)
+        onehot8[n, 0:32, :] = hat.astype(F8)
+
+        @pl.when(n == 0)
+        def _():
+            onehot[0:32, :] = hat.astype(BF16)
 
         reach = rows + 2 * HALO
         between = lax.broadcasted_iota(jnp.int32, (reach, slots), 0) - HALO
@@ -279,6 +299,9 @@
 
     def scattered(filter_ref, bands, first):
         acc[...] = jnp.zeros_like(acc)
+        peak = jnp.max(jnp.max(jnp.abs(q_now[...]), axis=0, keepdims=True), axis=1, keepdims=True)
+        peak = jnp.maximum(peak, 1e-30)
+        gain = (ROOM / c) / peak
 
         @pl.loop(0, bands)
         def _(n):
@@ -291,17 +314,17 @@
                 values = jnp.broadcast_to(bvals[n][:, None, :], (members, rows, slots))
                 spread[n] = values.reshape(flat, slots).astype(BF16)
 
-            factor = filter_ref[n] * q_now[pl.ds(n, 1), :]
+            factor = filter_ref[n] * (q_now[pl.ds(n, 1), :] * gain)
             value = spread[n].astype(F32).reshape(members, rows, slots) * factor[None]
-            high, low = halves(value.reshape(flat, slots))
             acc[...] += lax.dot_general(
-                jnp.concatenate([high, low], axis=0),
-                onehot[n],
+                thirds(value.reshape(flat, slots)),
+                onehot8[n],
                 (((1,), (1,)), ((), ())),
                 preferred_element_type=F32,
             )
 
-        return acc[:flat] + acc[flat:]
+        total = acc[:flat] + (1.0 / 16.0) * (acc[flat : 2 * flat] + (1.0 / 16.0) * acc[2 * flat :])
+        return total * (peak * (c / ROOM))
 
     def filtered(value, which):
         high, low = halves(value)
@@ -340,7 +363,7 @@
             vwide[:, j * BLOCK : (j + 1) * BLOCK] = jnp.concatenate([high, low], axis=0)
         vwide[:, cols:] = vwide[:, :PAD]
 
-        seen = dot(vwide[:, :cols], onehot[0])
+        seen = dot(vwide[:, :cols], onehot[...])
         hits_part = c * jnp.sum(
             chosen[...].astype(F32) * (seen[:flat] + seen[flat:]), axis=0, keepdims=True
         )
@@ -476,7 +499,8 @@
         pltpu.VMEM((NEAR, flat, slots), BF16),
         pltpu.VMEM((flat, slots), BF16),
         pltpu.VMEM((2 * flat, fine_cols), BF16),
-        pltpu.VMEM((NEAR, cols, slots), BF16),
+        pltpu.VMEM((cols, slots), BF16),
+        pltpu.VMEM((NEAR, cols, slots), F8),
         pltpu.VMEM((NEAR, rows, slots), F32),
         pltpu.VMEM((NEAR, rows, slots), F32),
         pltpu.VMEM((8, slots), F32),
@@ -486,7 +510,7 @@
         pltpu.VMEM((8, slots), F32),
         pltpu.VMEM((8, slots), F32),
         pltpu.VMEM((1, slots), F32),
-        pltpu.VMEM((2 * flat, cols), F32),
+        pltpu.VMEM((3 * flat, cols), F32),
         pltpu.VMEM((2 * flat, cols + 2 * PAD), BF16),
         pltpu.VMEM((2 * flat, cols + PAD), BF16),
         pltpu.VMEM((flat, cols), F32),

time: 97.8 us -> 94.1 us (0.962)
  Pallas kernels: 93.8 us -> 90.1 us
    pallas_call x1, Pallas kernels: 93.8 us -> 90.1 us  [on_device(): pl.pallas_call(functools.partial(body, n_mem, n_lat), out_shape=(jax.Shap...]
where the time goes in v4:
time: 94.1 us; the launch traced here: 93.9 us
  Pallas kernels  90.1 us (96%)
  local copies, waits for them, and re-layouts  2.49 us (3%)
  between operations  1.29 us (1%)
    pallas_call x1, Pallas kernels, on_device(): pl.pallas_call(functools.partial(body, n_mem, n_lat), out_shape=(jax.Shap...  90.1 us
    unnamed x4, local copies, waits for them, and re-layouts  2.49 us

profile of v4, /device:TPU:1, one launch (start us, length us, event | category | flops | bytes accessed | tf_op | source)
XLA Modules:
  0.0 93.9 jit_solution(11085891880146777443)
XLA Ops:
  1.3 90.1 %shard_map.95 = (f32[16,8,1024]{2,1,0:T(8,128)}, f32[16,128]{1,0:T(8,128)}) custom-call(s32[1,2048]{1,0:T(1,128)} %cells_ref.1, s32[1]{0:T(128)S(6)} %copy.12.count_ref, f32[1,2048]{1,0:T(1,128)} %innov_ref.1, f32[1,2048]{1,0:T(1,128)} %scale_ref.1, bf16[16,16,2048]{2,1,0:T(8,128)(2,1)} %pert_ref.1, bf16[256,256]{1,0:T(8,128)(2,1)} %constant.6.clone.sel_ref, ...), custom_call_target="tpu_custom_call" | custom-call | tf_op jit(solution)/shard_map/pallas_call | solution.py:531
  91.4 0.0 copy-start
  91.4 1.9 %copy.13 = f32[16,8,1024]{2,1,0:T(8,128)} copy(f32[16,8,1024]{2,1,0:T(8,128)} %get-tuple-element.4) | data formatting | bytes 1048576
  93.3 0.0 copy-done
  93.3 0.6 copy.14
Async XLA Ops:
  91.4 1.9 %copy-start = (f32[16,128]{1,0:T(8,128)S(1)}, f32[16,128]{1,0:T(8,128)}, u32[]{:S(2)}) copy-start(f32[16,128]{1,0:T(8,128)} %get-tuple-element.5) | copy-start | bytes 24580
